TPU v7x, 32 devices: a whole 2x2x4 slice. The times are simulated.
32 devices in a mesh: prow: 2 (over core), pcol: 16 (over z, y, x).
Axes of the slice: x: 2, y: 2, z: 4, core: 2. Of those that a mesh axis runs over, the one named last changes fastest.
Arguments:
- slab: float32 [1024, 98304], P('pcol', 'prow'), may hold values from -6 to 6
- vectors: float32 [98304, 512], P(('prow', 'pcol')), may hold values from -0.01953125 to 0.01953125
- tfactors: float32 [4, 128, 128], replicated, as said below
Outputs:
- transformed: float32 [1024, 98304], P('pcol', 'prow')
Inputs may be any that keep to these rules, and one draw needn't show every extreme that they name: Each tfactors[k] is upper triangular with diagonal entries between 1 and 2.
All inputs are finite; a program needn't handle non-finite values.
Results may differ from a plain program's by a relative error of at most 0.0001.
Values sent between devices are 32-bit elements; how exact they have to be, the bound alone decides.
A program may use at most 192 MiB of HBM per device.

v0:
```python
import jax
import jax.numpy as jnp
from jax import lax
from jax.sharding import PartitionSpec as P


def matmul(left, right):
    return jnp.dot(left, right, precision=lax.Precision.HIGHEST, preferred_element_type=jnp.float32)


def per_device(slab, vectors, tfactors):
    count = tfactors.shape[0]
    width = tfactors.shape[1]
    work = slab
    for k in reversed(range(count)):
        basis = lax.all_gather(vectors[:, k * width : (k + 1) * width], "pcol", axis=0, tiled=True)
        products = lax.psum(matmul(work, basis), "prow")
        work = work - matmul(matmul(products, tfactors[k].T), basis.T)
    return work


def solution(mesh):
    in_specs = (P("pcol", "prow"), P(("prow", "pcol"), None), P())
    out_specs = P("pcol", "prow")
    return jax.shard_map(
        per_device, mesh=mesh, in_specs=in_specs, out_specs=out_specs, check_vma=False
    )
```

profile of v0, /device:TPU:0, one launch (start us, length us, event | category | flops | bytes accessed | tf_op | source)
XLA Modules:
  0.0 1167.0 jit_solution(2960189961341196139)
XLA Ops:
  6.5 0.0 all-gather.5.cloned.1.call-start
  6.5 5.7 fusion.12
  12.2 0.0 all-gather.5.cloned.1.call-update
  12.3 0.0 all-gather.7.cloned.1.call-start
  12.3 0.7 all-gather.7.cloned.1.call-update
  13.0 0.0 all-gather.9.cloned.1.call-start
  13.1 0.7 all-gather.9.cloned.1.call-update
  13.7 0.0 all-gather.11.cloned.1.call-start
  13.8 0.5 all-gather.11.cloned.1.call-update
  14.3 0.0 copy-start
  14.3 272.0 %all-gather.5.cloned.1.call-done = f32[49152,128]{1,0:T(8,128)} async-done(((f32[3072,128]{1,0:T(8,128)}), f32[49152,128]{1,0:T(8,128)}) %all-gather.5.cloned.1.call-update) | async-done | bytes 25165840 | tf_op jit(solution)/shard_map/all_gather | solution.py:16
  286.3 20.5 %fusion.13 = f32[64,128]{1,0:T(8,128)S(1)} fusion(f32[64,49152]{1,0:T(8,128)} %param.3, f32[49152,128]{1,0:T(8,128)} %all-gather.5.cloned.1.call-done), kind=kOutput, calls=%fused_computation.17 | convolution fusion | flops 4831838208 | bytes 37781504 | tf_op jit(solution)/shard_map/dot_general | solution.py:8
  306.9 3.6 psum.28
  310.4 0.0 copy-done
  310.4 0.2 fusion.6
  310.7 34.0 %convolution_subtract_fusion.3 = f32[64,49152]{1,0:T(8,128)} fusion(f32[64,49152]{1,0:T(8,128)} %param.3, f32[64,128]{1,0:T(8,128)S(1)} %fusion.6, f32[49152,128]{1,0:T(8,128)} %all-gather.5.cloned.1.call-done), kind=kOutput, calls=%fused_computation.3 | convolution fusion | flops 4834983936 | bytes 50364416 | tf_op jit(solution)/shard_map/dot_general | solution.py:8
  344.7 213.9 %all-gather.7.cloned.1.call-done = f32[49152,128]{1,0:T(8,128)} async-done(((f32[3072,128]{1,0:T(8,128)}), f32[49152,128]{1,0:T(8,128)}) %all-gather.7.cloned.1.call-update) | async-done | bytes 25165840 | tf_op jit(solution)/shard_map/all_gather | solution.py:16
  558.6 20.5 %fusion.14 = f32[64,128]{1,0:T(8,128)S(1)} fusion(f32[64,49152]{1,0:T(8,128)} %convolution_subtract_fusion.3, f32[49152,128]{1,0:T(8,128)} %all-gather.7.cloned.1.call-done), kind=kOutput, calls=%fused_computation.18 | convolution fusion | flops 4831838208 | bytes 37781504 | tf_op jit(solution)/shard_map/dot_general | solution.py:8
  579.1 3.6 psum.29
  582.7 0.2 fusion.4
  583.0 34.1 %convolution_subtract_fusion.2 = f32[64,49152]{1,0:T(8,128)} fusion(f32[64,49152]{1,0:T(8,128)} %convolution_subtract_fusion.3, f32[64,128]{1,0:T(8,128)S(1)} %fusion.4, f32[49152,128]{1,0:T(8,128)} %all-gather.7.cloned.1.call-done), kind=kOutput, calls=%fused_computation.2 | convolution fusion | flops 4834983936 | bytes 50364416 | tf_op jit(solution)/shard_map/dot_general | solution.py:8
  617.0 213.8 %all-gather.9.cloned.1.call-done = f32[49152,128]{1,0:T(8,128)} async-done(((f32[3072,128]{1,0:T(8,128)}), f32[49152,128]{1,0:T(8,128)}) %all-gather.9.cloned.1.call-update) | async-done | bytes 25165840 | tf_op jit(solution)/shard_map/all_gather | solution.py:16
  830.8 20.5 %fusion.15 = f32[64,128]{1,0:T(8,128)S(1)} fusion(f32[64,49152]{1,0:T(8,128)} %convolution_subtract_fusion.2, f32[49152,128]{1,0:T(8,128)} %all-gather.9.cloned.1.call-done), kind=kOutput, calls=%fused_computation.19 | convolution fusion | flops 4831838208 | bytes 37781504 | tf_op jit(solution)/shard_map/dot_general | solution.py:8
  851.3 3.8 psum.30
  855.2 0.2 fusion.2
  855.4 34.0 %convolution_subtract_fusion.1 = f32[64,49152]{1,0:T(8,128)} fusion(f32[64,49152]{1,0:T(8,128)} %convolution_subtract_fusion.2, f32[64,128]{1,0:T(8,128)S(1)} %fusion.2, f32[49152,128]{1,0:T(8,128)} %all-gather.9.cloned.1.call-done), kind=kOutput, calls=%fused_computation.1 | convolution fusion | flops 4834983936 | bytes 50364416 | tf_op jit(solution)/shard_map/dot_general | solution.py:8
  889.4 213.5 %all-gather.11.cloned.1.call-done = f32[49152,128]{1,0:T(8,128)} async-done(((f32[3072,128]{1,0:T(8,128)}), f32[49152,128]{1,0:T(8,128)}) %all-gather.11.cloned.1.call-update) | async-done | bytes 25165840 | tf_op jit(solution)/shard_map/all_gather | solution.py:16
  1102.9 19.5 %fusion.16 = f32[64,128]{1,0:T(8,128)S(1)} fusion(f32[64,49152]{1,0:T(8,128)} %convolution_subtract_fusion.1, f32[49152,128]{1,0:T(8,128)} %all-gather.11.cloned.1.call-done), kind=kOutput, calls=%fused_computation.20 | convolution fusion | flops 4831838208 | bytes 37781504 | tf_op jit(solution)/shard_map/dot_general | solution.py:8
  1122.4 3.6 psum.31
  1126.0 0.2 fusion
  1126.3 34.0 %convolution_subtract_fusion = f32[64,49152]{1,0:T(8,128)} fusion(f32[64,49152]{1,0:T(8,128)} %convolution_subtract_fusion.1, f32[64,128]{1,0:T(8,128)S(1)} %fusion, f32[49152,128]{1,0:T(8,128)} %all-gather.11.cloned.1.call-done), kind=kOutput, calls=%fused_computation | convolution fusion | flops 4834983936 | bytes 50364416 | tf_op jit(solution)/shard_map/dot_general | solution.py:8
Async XLA Ops:
  6.5 279.8 %all-gather.5.cloned.1.call-start = ((), (), s32[]{:S(2)}) async-start(), calls=%async_computation | async-start | bytes 26738688 | tf_op jit(solution)/shard_map/all_gather | solution.py:16
  12.3 546.3 %all-gather.7.cloned.1.call-start = ((), (), s32[]{:S(2)}) async-start(), calls=%async_computation.1 | async-start | bytes 26738688 | tf_op jit(solution)/shard_map/all_gather | solution.py:16
  13.0 817.8 %all-gather.9.cloned.1.call-start = ((), (), s32[]{:S(2)}) async-start(), calls=%async_computation.2 | async-start | bytes 26738688 | tf_op jit(solution)/shard_map/all_gather | solution.py:16
  13.7 1089.1 %all-gather.11.cloned.1.call-start = ((), (), s32[]{:S(2)}) async-start(), calls=%async_computation.3 | async-start | bytes 26738688 | tf_op jit(solution)/shard_map/all_gather | solution.py:16
  14.3 296.1 %copy-start = (f32[4,128,128]{2,1,0:T(8,128)S(1)}, f32[4,128,128]{2,1,0:T(8,128)}, u32[]{:S(2)}) copy-start(f32[4,128,128]{2,1,0:T(8,128)} %param.5) | copy-start | bytes 786436
Sparse Core Ops, SparseCore 0:
  12.4 273.9 all-gather.4
  289.1 269.4 all-gather.6
  561.3 269.4 all-gather.8
  833.4 269.4 all-gather.10
where the time goes:
time: 1170 us
  waiting for transfers between devices  915 us (78%)
  matrix products  218 us (19%)
  blocking collectives  14.6 us (1%)
  between operations  13.4 us (1%)
    all_gather x4, waiting for transfers between devices, per_device(): lax.all_gather(vectors[:, k * width:(k + 1) * width], 'pcol', axis=0, til...  913 us
    dot_general x12, matrix products, matmul(): jnp.dot(left, right, precision=lax.Precision.HIGHEST, preferred_element_t...  218 us
  transfers between devices with their start and end apart: 4, of which 4 were waited for; matrix products, arithmetic and copies ran while one was open for 14% of the time, Pallas kernels for 0%

commit v1 on v0

v1 whole, which is shorter than its diff:
```python
import functools

import jax
import jax.numpy as jnp
from jax import lax
from jax.experimental import pallas as pl
from jax.experimental.pallas import tpu as pltpu
from jax.sharding import PartitionSpec as P

MESH = pl.DeviceIdType.MESH
GROUP = 4
CHUNKS = 4


def matmul(left, right, precision=lax.Precision.HIGHEST):
    return jnp.dot(left, right, precision=precision, preferred_element_type=jnp.float32)


def greet_all(count):
    row, me = lax.axis_index("prow"), lax.axis_index("pcol")
    barrier = pltpu.get_barrier_semaphore()
    for step in range(1, count):
        pl.semaphore_signal(barrier, inc=1, device_id=(row, lax.rem(me + step, count)), device_id_type=MESH)
    pl.semaphore_wait(barrier, count - 1)


def place_of(line, plane, piece):
    reach = line - 2
    return jnp.clip(plane, piece - reach, piece + reach)


def spread_kernel(line, slab_ref, vec_ref, xr, vall, xsend, xrecv, vright, vleft, vrecv, own_sem):
    count = line * GROUP
    row, me = lax.axis_index("prow"), lax.axis_index("pcol")
    z, q = me // GROUP, lax.rem(me, GROUP)
    depth = vec_ref.shape[0]
    part = depth // CHUNKS
    greet_all(count)

    def vcopy(source, chunk, to, src, sems):
        rows = pl.ds(chunk * part, part)
        return pltpu.make_async_remote_copy(
            src_ref=src.at[rows, :],
            dst_ref=vall.at[source, rows, :],
            send_sem=sems.at[source, chunk],
            recv_sem=vrecv.at[source, chunk],
            device_id=(row, to * GROUP + q),
            device_id_type=MESH,
        )

    for chunk in range(CHUNKS):
        @pl.when(z < line - 1)
        def _():
            vcopy(z, chunk, z + 1, vec_ref, vright).start()

        @pl.when(z > 0)
        def _():
            vcopy(z, chunk, z - 1, vec_ref, vleft).start()

    own = pltpu.make_async_copy(vec_ref, vall.at[z], own_sem)
    own.start()

    def xcopy(piece, step):
        other = lax.rem(q + step, GROUP)
        place = place_of(line, z, piece)
        slot = jnp.where(place == z, piece, line)
        columns = pl.ds(pl.multiple_of((piece * GROUP + other) * depth, 128), depth)
        return place, other, slot, columns

    def xremote(piece, step):
        place, other, slot, columns = xcopy(piece, step)
        return pltpu.make_async_remote_copy(
            src_ref=slab_ref.at[:, columns],
            dst_ref=xr.at[slot, q],
            send_sem=xsend.at[piece, step],
            recv_sem=xrecv.at[slot, q],
            device_id=(row, place * GROUP + other),
            device_id_type=MESH,
        )

    def xlocal(piece):
        _, _, _, columns = xcopy(piece, 0)
        return pltpu.make_async_copy(slab_ref.at[:, columns], xr.at[piece, q], xrecv.at[piece, q])

    def far(piece):
        return place_of(line, z, piece) != z

    for step in (1, 2, 3, 0):
        for piece in range(line):
            if step:
                xremote(piece, step).start()
            else:
                @pl.when(far(piece))
                def _():
                    xremote(piece, 0).start()

                @pl.when(jnp.logical_not(far(piece)))
                def _():
                    xlocal(piece).start()

    for distance in range(1, line - 1):
        for chunk in range(CHUNKS):
            @pl.when(z - distance >= 0)
            def _():
                source = z - distance
                vcopy(source, chunk, z, vall.at[source], vright).wait_recv()
                if distance + 1 <= line - 2:
                    @pl.when(z < line - 1)
                    def _():
                        vcopy(source, chunk, z + 1, vall.at[source], vright).start()

            @pl.when(z + distance <= line - 1)
            def _():
                source = z + distance
                vcopy(source, chunk, z, vall.at[source], vleft).wait_recv()
                if distance + 1 <= line - 2:
                    @pl.when(z > 0)
                    def _():
                        vcopy(source, chunk, z - 1, vall.at[source], vleft).start()

    own.wait()

    def xarrived(slot, other):
        pltpu.make_async_remote_copy(
            src_ref=xr.at[slot, other],
            dst_ref=xr.at[slot, other],
            send_sem=xsend.at[0, 0],
            recv_sem=xrecv.at[slot, other],
            device_id=(row, me),
            device_id_type=MESH,
        ).wait_recv()

    for piece in range(line):
        @pl.when(jnp.logical_not(far(piece)))
        def _():
            xlocal(piece).wait()
            for step in range(1, GROUP):
                xarrived(piece, lax.rem(q + step, GROUP))

    @pl.when(jnp.logical_or(z == 1, z == line - 2))
    def _():
        for other in range(GROUP):
            xarrived(line, other)

    for piece in range(line):
        for step in range(1, GROUP):
            xremote(piece, step).wait_send()

        @pl.when(far(piece))
        def _():
            xremote(piece, 0).wait_send()

    for distance in range(0, line - 2):
        for chunk in range(CHUNKS):
            @pl.when(jnp.logical_and(z - distance >= 0, z < line - 1))
            def _():
                vcopy(z - distance, chunk, z + 1, vec_ref, vright).wait_send()

            @pl.when(jnp.logical_and(z + distance <= line - 1, z > 0))
            def _():
                vcopy(z + distance, chunk, z - 1, vec_ref, vleft).wait_send()


def spread(line, slab, vectors):
    rows = slab.shape[0]
    depth, width = vectors.shape
    return pl.pallas_call(
        functools.partial(spread_kernel, line),
        out_shape=(
            jax.ShapeDtypeStruct((line + 1, GROUP, rows, depth), jnp.float32),
            jax.ShapeDtypeStruct((line, depth, width), jnp.float32),
        ),
        in_specs=[pl.BlockSpec(memory_space=pl.ANY)] * 2,
        out_specs=(pl.BlockSpec(memory_space=pl.ANY),) * 2,
        scratch_shapes=[
            pltpu.SemaphoreType.DMA((line, GROUP)),
            pltpu.SemaphoreType.DMA((line + 1, GROUP)),
            pltpu.SemaphoreType.DMA((line, CHUNKS)),
            pltpu.SemaphoreType.DMA((line, CHUNKS)),
            pltpu.SemaphoreType.DMA((line, CHUNKS)),
            pltpu.SemaphoreType.DMA,
        ],
        compiler_params=pltpu.CompilerParams(collective_id=0, has_side_effects=True),
        name="spread",
    )(slab, vectors)


def give_back_kernel(line, c_ref, out_ref, send, recv):
    count = line * GROUP
    row, me = lax.axis_index("prow"), lax.axis_index("pcol")
    z, q = me // GROUP, lax.rem(me, GROUP)
    depth = c_ref.shape[3]
    greet_all(count)

    def columns(piece, other):
        return pl.ds(pl.multiple_of((piece * GROUP + other) * depth, 128), depth)

    def remote(slot, piece, plane, other):
        return pltpu.make_async_remote_copy(
            src_ref=c_ref.at[slot, other],
            dst_ref=out_ref.at[:, columns(piece, q)],
            send_sem=send.at[slot, other],
            recv_sem=recv.at[piece, q],
            device_id=(row, plane * GROUP + other),
            device_id_type=MESH,
        )

    def local(piece):
        return pltpu.make_async_copy(c_ref.at[piece, q], out_ref.at[:, columns(piece, q)], recv.at[piece, q])

    def near(piece):
        return place_of(line, z, piece) == z

    helps = jnp.logical_or(z == 1, z == line - 2)
    far_plane = jnp.where(z == 1, 0, line - 1)
    far_piece = jnp.where(z == 1, line - 1, 0)

    @pl.when(helps)
    def _():
        for other in range(GROUP):
            remote(line, far_piece, far_plane, other).start()

    for step in (1, 2, 3, 0):
        for piece in range(line):
            @pl.when(near(piece))
            def _():
                if step:
                    remote(piece, piece, z, lax.rem(q + step, GROUP)).start()
                else:
                    local(piece).start()

    def arrived(piece, other):
        pltpu.make_async_remote_copy(
            src_ref=c_ref.at[0, 0],
            dst_ref=out_ref.at[:, columns(piece, other)],
            send_sem=send.at[0, 0],
            recv_sem=recv.at[piece, other],
            device_id=(row, me),
            device_id_type=MESH,
        ).wait_recv()

    for piece in range(line):
        for step in range(1, GROUP):
            arrived(piece, lax.rem(q + step, GROUP))

        @pl.when(near(piece))
        def _():
            local(piece).wait()

        @pl.when(jnp.logical_not(near(piece)))
        def _():
            arrived(piece, q)

    for piece in range(line):
        @pl.when(near(piece))
        def _():
            for step in range(1, GROUP):
                remote(piece, piece, z, lax.rem(q + step, GROUP)).wait_send()

    @pl.when(helps)
    def _():
        for other in range(GROUP):
            remote(line, far_piece, far_plane, other).wait_send()


def give_back(line, correction):
    _, _, rows, depth = correction.shape
    return pl.pallas_call(
        functools.partial(give_back_kernel, line),
        out_shape=jax.ShapeDtypeStruct((rows, line * GROUP * depth), jnp.float32),
        in_specs=[pl.BlockSpec(memory_space=pl.ANY)],
        out_specs=pl.BlockSpec(memory_space=pl.ANY),
        scratch_shapes=[
            pltpu.SemaphoreType.DMA((line + 1, GROUP)),
            pltpu.SemaphoreType.DMA((line, GROUP)),
        ],
        compiler_params=pltpu.CompilerParams(collective_id=1, has_side_effects=True),
        name="give_back",
    )(correction)


def per_device(line, slab, vectors, tfactors):
    count, width = tfactors.shape[0], tfactors.shape[1]
    rows = slab.shape[0]
    depth, total = vectors.shape
    z = lax.axis_index("pcol") // GROUP
    high = lax.Precision.HIGH

    gram = lax.psum(matmul(vectors.T, vectors, high), ("prow", "pcol"))
    xr, vall = spread(line, slab, vectors)
    xr = xr.reshape(line + 1, GROUP * rows, depth)

    own = jnp.zeros((GROUP * rows, total), jnp.float32)
    for piece in range(line):
        near = place_of(line, z, piece) == z
        own = own + jnp.where(near, matmul(xr[piece], vall[piece], high), 0.0)
    helps = jnp.logical_or(z == 1, z == line - 2)
    far_plane = jnp.where(z == 1, 0, line - 1)
    far_piece = jnp.where(z == 1, line - 1, 0)
    far_vectors = lax.dynamic_index_in_dim(vall, far_piece, 0, keepdims=False)
    extra = jnp.where(helps, matmul(xr[line], far_vectors, high), 0.0)

    products = jnp.zeros((line, GROUP * rows, total), jnp.float32)
    products = lax.dynamic_update_index_in_dim(products, own, z, 0)
    before = lax.dynamic_index_in_dim(products, far_plane, 0, keepdims=False)
    products = lax.dynamic_update_index_in_dim(products, jnp.where(helps, extra, before), far_plane, 0)
    products = lax.psum(products, ("prow", "pcol"))

    def weights(part):
        done = {}
        for k in reversed(range(count)):
            now = part[:, k * width : (k + 1) * width]
            for j in done:
                now = now - matmul(done[j], gram[j * width : (j + 1) * width, k * width : (k + 1) * width])
            done[k] = matmul(now, tfactors[k].T)
        return jnp.concatenate([done[k] for k in range(count)], axis=1)

    both = jnp.concatenate([
        lax.dynamic_index_in_dim(products, z, 0, keepdims=False),
        lax.dynamic_index_in_dim(products, far_plane, 0, keepdims=False),
    ])
    both = weights(both)
    w_own, w_far = both[: GROUP * rows], both[GROUP * rows :]
    parts = [matmul(w_own, vall[piece].T, high) for piece in range(line)]
    parts.append(matmul(w_far, far_vectors.T, high))
    correction = jnp.stack(parts).reshape(line + 1, GROUP, rows, depth)
    return slab - give_back(line, correction)


def solution(mesh):
    line = mesh.shape["pcol"] // GROUP
    in_specs = (P("pcol", "prow"), P(("prow", "pcol"), None), P())
    out_specs = P("pcol", "prow")
    return jax.shard_map(
        functools.partial(per_device, line), mesh=mesh, in_specs=in_specs, out_specs=out_specs, check_vma=False
    )
```

time: 1170 us -> 722 us (0.62)
  waiting for transfers between devices: 915 us -> 150 us
  Pallas kernels: 0 us -> 434 us
  matrix products: 218 us -> 86.5 us
  blocking collectives: 14.6 us -> 0 us
  other arithmetic: 0 us -> 14 us
    all_gather x4 -> x0, waiting for transfers between devices: 913 us -> none  [per_device(): lax.all_gather(vectors[:, k * width:(k + 1) * width], 'pcol', axis=0, til...]
    pallas_call x0 -> x2, Pallas kernels: none -> 434 us  [the longest x1 279 us: spread(): pl.pallas_call(functools.partial(spread_kernel, line), out_shape=(jax.Sha...]
    psum x0 -> x1, waiting for transfers between devices: none -> 150 us  [per_device(): products = lax.psum(products, ('prow', 'pcol'))]
    dot_general x12 -> x21, matrix products: 218 us -> 86.5 us  [matmul(): jnp.dot(left, right, precision=precision, preferred_element_type=jnp.floa...]
    psum x4 -> x0, blocking collectives: 14.6 us -> none  [per_device(): products = lax.psum(matmul(work, basis), 'prow')]
    sub x0 -> x1, other arithmetic: none -> 13.9 us  [per_device(): return slab - give_back(line, correction)]
  transfers between devices with their start and end apart: 4 -> 1, of which waited for: 4 -> 1; matrix products, arithmetic and copies ran while one was open for 14% -> 0% of each run, Pallas kernels for 0% -> 0%
where the time goes in v1:
time: 722 us; the launch traced here: 713 us
  Pallas kernels  434 us (60%)
  waiting for transfers between devices  150 us (21%)
  matrix products  86.5 us (12%)
  local copies, waits for them, and re-layouts  14.3 us (2%)
  between operations  14.1 us (2%)
  other arithmetic  14 us (2%)
    pallas_call x1, Pallas kernels, spread(): pl.pallas_call(functools.partial(spread_kernel, line), out_shape=(jax.Sha...  279 us
    pallas_call x1, Pallas kernels, give_back(): pl.pallas_call(functools.partial(give_back_kernel, line), out_shape=jax.S...  155 us
    psum x1, waiting for transfers between devices, per_device(): products = lax.psum(products, ('prow', 'pcol'))  150 us
    dot_general x21, matrix products, matmul(): jnp.dot(left, right, precision=precision, preferred_element_type=jnp.floa...  86.5 us
  transfers between devices with their start and end apart: 1, of which 1 were waited for; matrix products, arithmetic and copies ran while one was open for 0% of the time, Pallas kernels for 0%

profile of v1, /device:TPU:0, one launch (start us, length us, event | category | flops | bytes accessed | tf_op | source)
XLA Modules:
  0.0 713.0 jit_solution(16042292631192386047)
XLA Ops:
  6.5 14.8 %fusion.126 = f32[512,512]{1,0:T(8,128)} fusion(f32[3072,512]{1,0:T(8,128)} %vec_ref.1), kind=kOutput, calls=%fused_computation.96 | convolution fusion | flops 4831838208 | bytes 7340032 | tf_op jit(solution)/shard_map/dot_general | solution.py:16
  21.4 278.7 %spread.1 = (f32[5,4,64,3072]{3,2,1,0:T(8,128)}, f32[4,3072,512]{2,1,0:T(8,128)}) custom-call(f32[64,49152]{1,0:T(8,128)} %slab_ref.1, f32[3072,512]{1,0:T(8,128)} %vec_ref.1), custom_call_target="tpu_custom_call" | custom-call | tf_op jit(solution)/shard_map/spread/pallas_call | solution.py:167
  300.1 10.9 %fusion.124 = (f32[1,4,64,3072]{3,2,1,0:T(8,128)}, f32[1,4,64,3072]{3,2,1,0:T(8,128)}, f32[1,4,64,3072]{3,2,1,0:T(8,128)}, f32[1,4,64,3072]{3,2,1,0:T(8,128)S(1)}, f32[1,4,64,3072]{3,2,1,0:T(8,128)}) fusion(f32[5,4,64,3072]{3,2,1,0:T(8,128)} %get-tuple-element.7), kind=kLoop, calls=%fused_computation.94 | loop fusion | bytes 31457280 | tf_op jit(solution)/shard_map/slice | solution.py:301
  311.0 5.3 fusion.66
  316.3 6.9 fusion.63
  323.3 5.9 fusion.72
  329.2 0.2 broadcast_in_dim.19
  329.5 3.4 fusion.84
  332.9 3.5 fusion.96
  336.4 1.3 copy-done.4
  337.8 150.2 %all-reduce.3.cloned.1.call-done = (f32[4,256,512]{2,1,0:T(8,128)}, f32[512,512]{1,0:T(8,128)}) async-done(((f32[4,256,512]{2,1,0:T(8,128)}, f32[512,512]{1,0:T(8,128)}), (f32[4,256,512]{2,1,0:T(8,128)}, f32[512,512]{1,0:T(8,128)})) %all-reduce.3.cloned.1.call-update) | async-done | bytes 3145744 | tf_op jit(solution)/shard_map/psum | solution.py:307
  488.0 1.3 dynamic-slice_bitcast_fusion
  489.2 0.4 fusion.102
  489.6 1.4 convolution_subtract_fusion.5
  491.1 1.4 convolution_subtract_fusion.4
  492.5 1.4 convolution_subtract_fusion.2
  494.0 0.4 fusion.114
  494.4 1.4 convolution_subtract_fusion.3
  495.8 1.4 convolution_subtract_fusion.1
  497.2 0.4 fusion.112
  497.6 1.4 convolution_subtract_fusion
  499.1 0.4 fusion.110
  499.5 0.1 pad_maximum_fusion
  499.6 0.2 copy.9
  499.8 7.5 %fusion.33 = f32[5,4,64,3072]{3,2,1,0:T(8,128)} fusion(f32[4,64,512]{2,1,0:T(8,128)S(1)} %bitcast.150, f32[4,3072,512]{2,1,0:T(8,128)} %get-tuple-element.8), kind=kOutput, calls=%fused_computation.31 | convolution fusion | flops 2415919104 | bytes 9961472 | tf_op jit(solution)/shard_map/dot_general | solution.py:16
  507.3 7.3 %fusion.39 = f32[5,4,64,3072]{3,2,1,0:T(8,128)} fusion(f32[5,4,64,3072]{3,2,1,0:T(8,128)} %fusion.33, f32[4,64,512]{2,1,0:T(8,128)S(1)} %bitcast.151, f32[4,3072,512]{2,1,0:T(8,128)} %get-tuple-element.8), kind=kOutput, calls=%fused_computation.33 | convolution fusion | flops 2415919104 | bytes 9961472 | tf_op jit(solution)/shard_map/dot_general | solution.py:16
  514.5 7.2 %fusion.45 = f32[5,4,64,3072]{3,2,1,0:T(8,128)} fusion(f32[5,4,64,3072]{3,2,1,0:T(8,128)} %fusion.39, f32[4,64,512]{2,1,0:T(8,128)S(1)} %bitcast.152, f32[4,3072,512]{2,1,0:T(8,128)} %get-tuple-element.8), kind=kOutput, calls=%fused_computation.35 | convolution fusion | flops 2415919104 | bytes 9961472 | tf_op jit(solution)/shard_map/dot_general | solution.py:16
  521.7 7.3 %fusion.51 = f32[5,4,64,3072]{3,2,1,0:T(8,128)} fusion(f32[5,4,64,3072]{3,2,1,0:T(8,128)} %fusion.45, f32[4,64,512]{2,1,0:T(8,128)S(1)} %bitcast.153, f32[4,3072,512]{2,1,0:T(8,128)} %get-tuple-element.8), kind=kOutput, calls=%fused_computation.37 | convolution fusion | flops 2415919104 | bytes 9961472 | tf_op jit(solution)/shard_map/dot_general | solution.py:16
  529.0 0.2 copy.10
  529.2 7.4 %fusion.57.c_ref = f32[5,4,64,3072]{3,2,1,0:T(8,128)} fusion(f32[5,4,64,3072]{3,2,1,0:T(8,128)} %fusion.51, f32[4,64,512]{2,1,0:T(8,128)S(1)} %bitcast.159, f32[4,3072,512]{2,1,0:T(8,128)} %get-tuple-element.8, s32[]{:T(128)S(6)} %select_n.74), kind=kOutput, calls=%fused_computation.39 | convolution fusion | flops 2415919104 | bytes 9961476 | tf_op jit(solution)/shard_map/dot_general | solution.py:16
  536.6 155.2 %give_back.1 = f32[64,49152]{1,0:T(8,128)} custom-call(f32[5,4,64,3072]{3,2,1,0:T(8,128)} %fusion.57.c_ref), custom_call_target="tpu_custom_call" | custom-call | tf_op jit(solution)/shard_map/give_back/pallas_call | solution.py:268
  691.8 13.9 %sub.32 = f32[64,49152]{1,0:T(8,128)} subtract(f32[64,49152]{1,0:T(8,128)} %slab_ref.1, f32[64,49152]{1,0:T(8,128)} %give_back.1) | non-fusion elementwise | flops 3145728 | bytes 37748736 | tf_op jit(solution)/shard_map/sub | solution.py:327
  (15 shorter events, 0.2 us)
Async XLA Ops:
  6.5 481.4 %all-reduce.3.cloned.1.call-start = ((), (), s32[]{:S(2)}) async-start(), calls=%async_computation | async-start | bytes 6291456 | tf_op jit(solution)/shard_map/psum | solution.py:307
  311.0 12.2 %copy-start.3 = (f32[1,4,64,3072]{3,2,1,0:T(8,128)S(1)}, f32[1,4,64,3072]{3,2,1,0:T(8,128)}, u32[]{:S(2)}) copy-start(f32[1,4,64,3072]{3,2,1,0:T(8,128)} %get-tuple-element.13) | copy-start | bytes 9437188
  311.0 18.5 %copy-start = (f32[4,3072,512]{2,1,0:T(8,128)S(1)}, f32[4,3072,512]{2,1,0:T(8,128)}, u32[]{:S(2)}) copy-start(f32[4,3072,512]{2,1,0:T(8,128)} %get-tuple-element.8) | copy-start | bytes 75497472
  323.3 6.2 copy-start.2
  329.5 3.4 copy-start.1
  332.9 156.3 %copy-start.5 = (f32[4,128,128]{2,1,0:T(8,128)S(1)}, f32[4,128,128]{2,1,0:T(8,128)}, u32[]{:S(2)}) copy-start(f32[4,128,128]{2,1,0:T(8,128)} %param.5) | copy-start | bytes 786436
  336.4 1.3 copy-start.4
Sparse Core Ops, SparseCore 0:
  337.9 150.0 all-reduce.2

commit v2 on v1

--- a/solution.py
+++ b/solution.py
@@ -185,19 +185,170 @@
     )(slab, vectors)
 
 
-def give_back_kernel(line, c_ref, out_ref, send, recv):
-    count = line * GROUP
+def split(value):
+    coarse = value.astype(jnp.bfloat16)
+    return coarse, (value - coarse.astype(jnp.float32)).astype(jnp.bfloat16)
+
+
+def across(left, right):
+    return lax.dot_general(left, right, (((1,), (1,)), ((), ())), preferred_element_type=jnp.float32)
+
+
+def finish_kernel(
+    line, lanes, x_ref, v_ref, y_ref, gram_ref, t_ref, out_ref,
+    xbuf, vbuf, inbox, total, wbox, wsplit,
+    xload, vload, ysend, yrecv, wsend, wrecv, send, recv,
+):
     row, me = lax.axis_index("prow"), lax.axis_index("pcol")
     z, q = me // GROUP, lax.rem(me, GROUP)
-    depth = c_ref.shape[3]
-    greet_all(count)
+    members = lanes * GROUP
+    mine = row * GROUP + q
+    blocks, width = t_ref.shape[0], t_ref.shape[1]
+    rows, depth = xbuf.shape[2], xbuf.shape[3]
+    share = GROUP * rows // members
+
+    helps = jnp.logical_or(z == 1, z == line - 2)
+    ends = jnp.logical_or(z == 0, z == line - 1)
+    low = z <= 1
+    far_plane = jnp.where(low, 0, line - 1)
+    far_piece = jnp.where(low, line - 1, 0)
+    help_plane = jnp.where(low, 1, line - 2)
+    partner = jnp.where(ends, help_plane, far_plane)
+
+    def device(plane, member):
+        return (member // GROUP, plane * GROUP + lax.rem(member, GROUP))
+
+    def others():
+        return [lax.rem(mine + step, members) for step in range(1, members)]
+
+    for slot in range(line + 1):
+        pltpu.make_async_copy(x_ref.at[slot], xbuf.at[slot], xload.at[slot]).start()
+    for piece in range(line):
+        pltpu.make_async_copy(v_ref.at[piece], vbuf.at[piece], vload.at[piece]).start()
+
+    barrier = pltpu.get_barrier_semaphore()
+    for other in others():
+        pl.semaphore_signal(barrier, inc=1, device_id=device(z, other), device_id_type=MESH)
+
+    @pl.when(jnp.logical_or(helps, ends))
+    def _():
+        for other in range(members):
+            pl.semaphore_signal(barrier, inc=1, device_id=device(partner, other), device_id_type=MESH)
+
+    pl.semaphore_wait(barrier, members - 1 + jnp.where(jnp.logical_or(helps, ends), members, 0))
+
+    def strip(member):
+        return pl.ds(pl.multiple_of(member * share, share), share)
+
+    def ycopy(kind, plane, member):
+        return pltpu.make_async_remote_copy(
+            src_ref=y_ref.at[kind, strip(member), :],
+            dst_ref=inbox.at[kind * members + mine],
+            send_sem=ysend.at[kind * members + member],
+            recv_sem=yrecv.at[kind * members + mine],
+            device_id=device(plane, member),
+            device_id_type=MESH,
+        )
+
+    def yarrived(index):
+        pltpu.make_async_remote_copy(
+            src_ref=inbox.at[index],
+            dst_ref=inbox.at[index],
+            send_sem=ysend.at[0],
+            recv_sem=yrecv.at[index],
+            device_id=(row, me),
+            device_id_type=MESH,
+        ).wait_recv()
+
+    @pl.when(helps)
+    def _():
+        for other in range(members):
+            ycopy(1, far_plane, other).start()
+
+    for other in others():
+        ycopy(0, z, other).start()
+
+    total[...] = y_ref[0, strip(mine), :]
+    for other in others():
+        yarrived(other)
+        total[...] += inbox[other]
+
+    @pl.when(ends)
+    def _():
+        for other in range(members):
+            yarrived(members + other)
+            total[...] += inbox[members + other]
+
+    done = {}
+    for k in reversed(range(blocks)):
+        now = total[:, k * width : (k + 1) * width]
+        for j in done:
+            now = now - matmul(done[j], gram_ref[j * width : (j + 1) * width, k * width : (k + 1) * width])
+        done[k] = lax.dot_general(
+            now, t_ref[k], (((1,), (1,)), ((), ())),
+            precision=lax.Precision.HIGHEST, preferred_element_type=jnp.float32,
+        )
+    for k in range(blocks):
+        wbox[0, strip(mine), k * width : (k + 1) * width] = done[k]
+
+    def wcopy(kind, plane, member):
+        return pltpu.make_async_remote_copy(
+            src_ref=wbox.at[0, strip(mine), :],
+            dst_ref=wbox.at[kind, strip(mine), :],
+            send_sem=wsend.at[kind * members + member],
+            recv_sem=wrecv.at[kind * members + mine],
+            device_id=device(plane, member),
+            device_id_type=MESH,
+        )
+
+    def warrived(kind, member):
+        pltpu.make_async_remote_copy(
+            src_ref=wbox.at[kind, strip(member), :],
+            dst_ref=wbox.at[kind, strip(member), :],
+            send_sem=wsend.at[0],
+            recv_sem=wrecv.at[kind * members + member],
+            device_id=(row, me),
+            device_id_type=MESH,
+        ).wait_recv()
+
+    @pl.when(ends)
+    def _():
+        for other in range(members):
+            wcopy(1, help_plane, other).start()
+
+    for other in others():
+        wcopy(0, z, other).start()
+
+    def xarrive(slot):
+        pltpu.make_async_copy(x_ref.at[slot], xbuf.at[slot], xload.at[slot]).wait()
+
+    for slot in range(line + 1):
+        xarrive(slot)
+    for piece in range(line):
+        pltpu.make_async_copy(v_ref.at[piece], vbuf.at[piece], vload.at[piece]).wait()
+
+    tile = 512 if depth % 512 == 0 else depth
+
+    def update(slot, piece, kind):
+        def body(index, carry):
+            span = pl.ds(pl.multiple_of(index * tile, tile), tile)
+            coarse, fine = split(vbuf[piece, span, :])
+            first, second = wsplit[2 * kind], wsplit[2 * kind + 1]
+            change = across(first, coarse) + (across(second, coarse) + across(first, fine))
+            for group in range(GROUP):
+                xbuf[slot, group, :, span] = (
+                    xbuf[slot, group, :, span] - change[group * rows : (group + 1) * rows]
+                )
+            return carry
+
+        lax.fori_loop(0, depth // tile, body, 0)
 
     def columns(piece, other):
         return pl.ds(pl.multiple_of((piece * GROUP + other) * depth, 128), depth)
 
     def remote(slot, piece, plane, other):
         return pltpu.make_async_remote_copy(
-            src_ref=c_ref.at[slot, other],
+            src_ref=xbuf.at[slot, other],
             dst_ref=out_ref.at[:, columns(piece, q)],
             send_sem=send.at[slot, other],
             recv_sem=recv.at[piece, q],
@@ -206,32 +357,36 @@
         )
 
     def local(piece):
-        return pltpu.make_async_copy(c_ref.at[piece, q], out_ref.at[:, columns(piece, q)], recv.at[piece, q])
+        return pltpu.make_async_copy(xbuf.at[piece, q], out_ref.at[:, columns(piece, q)], recv.at[piece, q])
 
     def near(piece):
         return place_of(line, z, piece) == z
 
-    helps = jnp.logical_or(z == 1, z == line - 2)
-    far_plane = jnp.where(z == 1, 0, line - 1)
-    far_piece = jnp.where(z == 1, line - 1, 0)
-
-    @pl.when(helps)
-    def _():
-        for other in range(GROUP):
-            remote(line, far_piece, far_plane, other).start()
-
-    for step in (1, 2, 3, 0):
-        for piece in range(line):
-            @pl.when(near(piece))
+    for other in others():
+        warrived(0, other)
+    wsplit[0], wsplit[1] = split(wbox[0])
+
+    for piece in range(line):
+        @pl.when(near(piece))
+        def _():
+            update(piece, piece, 0)
+            for step in (1, 2, 3):
+                remote(piece, piece, z, lax.rem(q + step, GROUP)).start()
+            local(piece).start()
+
+        if piece == 0:
+            @pl.when(helps)
             def _():
-                if step:
-                    remote(piece, piece, z, lax.rem(q + step, GROUP)).start()
-                else:
-                    local(piece).start()
+                for other in range(members):
+                    warrived(1, other)
+                wsplit[2], wsplit[3] = split(wbox[1])
+                update(line, far_piece, 1)
+                for other in range(GROUP):
+                    remote(line, far_piece, far_plane, other).start()
 
     def arrived(piece, other):
         pltpu.make_async_remote_copy(
-            src_ref=c_ref.at[0, 0],
+            src_ref=xbuf.at[0, 0],
             dst_ref=out_ref.at[:, columns(piece, other)],
             send_sem=send.at[0, 0],
             recv_sem=recv.at[piece, other],
@@ -246,91 +401,90 @@
         @pl.when(near(piece))
         def _():
             local(piece).wait()
-
-        @pl.when(jnp.logical_not(near(piece)))
-        def _():
-            arrived(piece, q)
-
-    for piece in range(line):
-        @pl.when(near(piece))
-        def _():
             for step in range(1, GROUP):
                 remote(piece, piece, z, lax.rem(q + step, GROUP)).wait_send()
 
+        @pl.when(jnp.logical_not(near(piece)))
+        def _():
+            arrived(piece, q)
+
+    for other in others():
+        ycopy(0, z, other).wait_send()
+        wcopy(0, z, other).wait_send()
+
+    @pl.when(ends)
+    def _():
+        for other in range(members):
+            wcopy(1, help_plane, other).wait_send()
+
     @pl.when(helps)
     def _():
+        for other in range(members):
+            ycopy(1, far_plane, other).wait_send()
         for other in range(GROUP):
             remote(line, far_piece, far_plane, other).wait_send()
 
 
-def give_back(line, correction):
-    _, _, rows, depth = correction.shape
+def finish(line, lanes, x, v, y, gram, tfactors):
+    _, _, rows, depth = x.shape
+    total = v.shape[2]
+    members = lanes * GROUP
+    share = GROUP * rows // members
+    dma = pltpu.SemaphoreType.DMA
     return pl.pallas_call(
-        functools.partial(give_back_kernel, line),
+        functools.partial(finish_kernel, line, lanes),
         out_shape=jax.ShapeDtypeStruct((rows, line * GROUP * depth), jnp.float32),
-        in_specs=[pl.BlockSpec(memory_space=pl.ANY)],
+        in_specs=[pl.BlockSpec(memory_space=pl.ANY)] * 2 + [pl.BlockSpec(memory_space=pltpu.VMEM)] * 3,
         out_specs=pl.BlockSpec(memory_space=pl.ANY),
         scratch_shapes=[
-            pltpu.SemaphoreType.DMA((line + 1, GROUP)),
-            pltpu.SemaphoreType.DMA((line, GROUP)),
+            pltpu.VMEM(x.shape, jnp.float32),
+            pltpu.VMEM(v.shape, jnp.float32),
+            pltpu.VMEM((2 * members, share, total), jnp.float32),
+            pltpu.VMEM((share, total), jnp.float32),
+            pltpu.VMEM((2, GROUP * rows, total), jnp.float32),
+            pltpu.VMEM((4, GROUP * rows, total), jnp.bfloat16),
+            dma((line + 1,)),
+            dma((line,)),
+            dma((2 * members,)),
+            dma((2 * members,)),
+            dma((2 * members,)),
+            dma((2 * members,)),
+            dma((line + 1, GROUP)),
+            dma((line, GROUP)),
         ],
-        compiler_params=pltpu.CompilerParams(collective_id=1, has_side_effects=True),
-        name="give_back",
-    )(correction)
-
-
-def per_device(line, slab, vectors, tfactors):
-    count, width = tfactors.shape[0], tfactors.shape[1]
+        compiler_params=pltpu.CompilerParams(
+            collective_id=1, has_side_effects=True, vmem_limit_bytes=60 * 1024 * 1024
+        ),
+        name="finish",
+    )(x, v, y, gram, tfactors)
+
+
+def per_device(line, lanes, slab, vectors, tfactors):
     rows = slab.shape[0]
     depth, total = vectors.shape
     z = lax.axis_index("pcol") // GROUP
     high = lax.Precision.HIGH
 
     gram = lax.psum(matmul(vectors.T, vectors, high), ("prow", "pcol"))
-    xr, vall = spread(line, slab, vectors)
-    xr = xr.reshape(line + 1, GROUP * rows, depth)
+    blocks, vall = spread(line, slab, vectors)
+    xr = blocks.reshape(line + 1, GROUP * rows, depth)
 
     own = jnp.zeros((GROUP * rows, total), jnp.float32)
     for piece in range(line):
         near = place_of(line, z, piece) == z
         own = own + jnp.where(near, matmul(xr[piece], vall[piece], high), 0.0)
-    helps = jnp.logical_or(z == 1, z == line - 2)
-    far_plane = jnp.where(z == 1, 0, line - 1)
-    far_piece = jnp.where(z == 1, line - 1, 0)
+    far_piece = jnp.where(z <= 1, line - 1, 0)
     far_vectors = lax.dynamic_index_in_dim(vall, far_piece, 0, keepdims=False)
-    extra = jnp.where(helps, matmul(xr[line], far_vectors, high), 0.0)
-
-    products = jnp.zeros((line, GROUP * rows, total), jnp.float32)
-    products = lax.dynamic_update_index_in_dim(products, own, z, 0)
-    before = lax.dynamic_index_in_dim(products, far_plane, 0, keepdims=False)
-    products = lax.dynamic_update_index_in_dim(products, jnp.where(helps, extra, before), far_plane, 0)
-    products = lax.psum(products, ("prow", "pcol"))
-
-    def weights(part):
-        done = {}
-        for k in reversed(range(count)):
-            now = part[:, k * width : (k + 1) * width]
-            for j in done:
-                now = now - matmul(done[j], gram[j * width : (j + 1) * width, k * width : (k + 1) * width])
-            done[k] = matmul(now, tfactors[k].T)
-        return jnp.concatenate([done[k] for k in range(count)], axis=1)
-
-    both = jnp.concatenate([
-        lax.dynamic_index_in_dim(products, z, 0, keepdims=False),
-        lax.dynamic_index_in_dim(products, far_plane, 0, keepdims=False),
-    ])
-    both = weights(both)
-    w_own, w_far = both[: GROUP * rows], both[GROUP * rows :]
-    parts = [matmul(w_own, vall[piece].T, high) for piece in range(line)]
-    parts.append(matmul(w_far, far_vectors.T, high))
-    correction = jnp.stack(parts).reshape(line + 1, GROUP, rows, depth)
-    return slab - give_back(line, correction)
+    extra = matmul(xr[line], far_vectors, high)
+    return finish(line, lanes, blocks, vall, jnp.stack([own, extra]), gram, tfactors)
 
 
 def solution(mesh):
     line = mesh.shape["pcol"] // GROUP
+    lanes = mesh.shape["prow"]
     in_specs = (P("pcol", "prow"), P(("prow", "pcol"), None), P())
     out_specs = P("pcol", "prow")
     return jax.shard_map(
-        functools.partial(per_device, line), mesh=mesh, in_specs=in_specs, out_specs=out_specs, check_vma=False
+        functools.partial(per_device, line, lanes),
+        mesh=mesh, in_specs=in_specs, out_specs=out_specs, check_vma=False,
     )

time: 722 us -> 560 us (0.78); the launches traced: 713 us -> 559 us
  waiting for transfers between devices: 150 us -> 0.02 us
  Pallas kernels: 434 us -> 480 us
  matrix products: 86.5 us -> 44 us
  other arithmetic: 14 us -> 1.04 us
    psum x1, waiting for transfers between devices: 150 us -> 0.01 us  [per_device(): gram = lax.psum(matmul(vectors.T, vectors, high), ('prow', 'pcol'))]
    dot_general x21 -> x6, matrix products: 86.5 us -> 44 us  [matmul(): jnp.dot(left, right, precision=precision, preferred_element_type=jnp.floa...]
    pallas_call x1, Pallas kernels: 155 us -> 188 us  [finish(): pl.pallas_call(functools.partial(finish_kernel, line, lanes), out_shape=j...]
    sub x1 -> x0, other arithmetic: 13.9 us -> none  [per_device(): return slab - give_back(line, correction)]
    pallas_call x1, Pallas kernels: 279 us -> 292 us  [spread(): pl.pallas_call(functools.partial(spread_kernel, line), out_shape=(jax.Sha...]
    unnamed x12 -> x9, local copies, waits for them, and re-layouts: 1.34 us -> 10.3 us
  transfers between devices with their start and end apart: 1 -> 1, of which waited for: 1 -> 0; matrix products, arithmetic and copies ran while one was open for 0% -> 7% of each run, Pallas kernels for 0% -> 52%
where the time goes in v2:
time: 560 us; the launch traced here: 559 us
  Pallas kernels  480 us (86%)
  matrix products  44 us (8%)
  local copies, waits for them, and re-layouts  21.2 us (4%)
  between operations  13.5 us (2%)
    pallas_call x1, Pallas kernels, spread(): pl.pallas_call(functools.partial(spread_kernel, line), out_shape=(jax.Sha...  292 us
    pallas_call x1, Pallas kernels, finish(): pl.pallas_call(functools.partial(finish_kernel, line, lanes), out_shape=j...  188 us
    dot_general x6, matrix products, matmul(): jnp.dot(left, right, precision=precision, preferred_element_type=jnp.floa...  44 us
  transfers between devices with their start and end apart: 1, of which 0 were waited for; matrix products, arithmetic and copies ran while one was open for 7% of the time, Pallas kernels for 52%

profile of v2, /device:TPU:0, one launch (start us, length us, event | category | flops | bytes accessed | tf_op | source)
XLA Modules:
  0.0 559.4 jit_solution(10286229756900709971)
XLA Ops:
  6.5 0.0 all-reduce.2.cloned.1.call-start
  6.5 14.8 %fusion.44 = f32[512,512]{1,0:T(8,128)} fusion(f32[3072,512]{1,0:T(8,128)} %vec_ref.1), kind=kOutput, calls=%fused_computation.27 | convolution fusion | flops 4831838208 | bytes 7340032 | tf_op jit(solution)/shard_map/dot_general | solution.py:16
  21.3 0.0 all-reduce.2.cloned.1.call-update
  21.4 291.8 %spread.1 = (f32[5,4,64,3072]{3,2,1,0:T(8,128)}, f32[4,3072,512]{2,1,0:T(8,128)}) custom-call(f32[64,49152]{1,0:T(8,128)} %slab_ref.1, f32[3072,512]{1,0:T(8,128)} %vec_ref.1), custom_call_target="tpu_custom_call" | custom-call | tf_op jit(solution)/shard_map/spread/pallas_call | solution.py:167
  313.2 10.9 %fusion.43 = (f32[1,4,64,3072]{3,2,1,0:T(8,128)}, f32[1,4,64,3072]{3,2,1,0:T(8,128)S(1)}, f32[1,4,64,3072]{3,2,1,0:T(8,128)}, f32[1,4,64,3072]{3,2,1,0:T(8,128)}, f32[1,4,64,3072]{3,2,1,0:T(8,128)}) fusion(f32[5,4,64,3072]{3,2,1,0:T(8,128)} %get-tuple-element.7.x_ref), kind=kLoop, calls=%fused_computation.26 | loop fusion | bytes 31457280 | tf_op jit(solution)/shard_map/slice | solution.py:475
  324.1 0.0 copy-start.2
  324.1 6.3 %fusion.24 = f32[256,512]{1,0:T(8,128)S(1)} fusion(f32[256,3072]{1,0:T(8,128)} %bitcast.50, f32[4,3072,512]{2,1,0:T(8,128)} %get-tuple-element.8.v_ref, pred[]{:T(512)S(6)} %eq.13), kind=kOutput, calls=%fused_computation.18 | convolution fusion | flops 2416050176 | bytes 9961473 | tf_op jit(solution)/shard_map/dot_general | solution.py:16
  330.4 0.0 copy-start.1
  330.4 0.0 copy-done.2
  330.4 5.4 fusion.21
  335.9 0.0 copy-start
  335.9 0.0 copy-done.1
  335.9 5.6 %fusion.30 = f32[256,512]{1,0:T(8,128)S(1)} fusion(f32[256,512]{1,0:T(8,128)S(1)} %fusion.21, f32[256,3072]{1,0:T(8,128)S(1)} %bitcast.52, f32[4,3072,512]{2,1,0:T(8,128)} %get-tuple-element.8.v_ref, pred[]{:T(512)S(6)} %eq.14), kind=kOutput, calls=%fused_computation.20 | convolution fusion | flops 2416181248 | bytes 10485761 | tf_op jit(solution)/shard_map/dot_general | solution.py:16
  341.5 0.0 copy-done
  341.5 6.6 %fusion.39 = f32[1,256,512]{2,1,0:T(8,128)} fusion(f32[256,512]{1,0:T(8,128)S(1)} %fusion.30, f32[256,3072]{1,0:T(8,128)S(1)} %bitcast.51, f32[4,3072,512]{2,1,0:T(8,128)} %get-tuple-element.8.v_ref, pred[]{:T(512)S(6)} %eq.15), kind=kOutput, calls=%fused_computation.23 | convolution fusion | flops 2416181248 | bytes 10485761 | tf_op jit(solution)/shard_map/dot_general | solution.py:16
  348.1 0.0 copy-start.3
  348.1 5.2 fusion.15
  353.4 0.0 copy-done.3
  353.4 1.0 pad_maximum_fusion.y_ref
  354.4 0.0 all-reduce.2.cloned.1.call-done.gram_ref
  354.4 187.8 %finish.1 = f32[64,49152]{1,0:T(8,128)} custom-call(f32[5,4,64,3072]{3,2,1,0:T(8,128)} %get-tuple-element.7.x_ref, f32[4,3072,512]{2,1,0:T(8,128)} %get-tuple-element.8.v_ref, f32[2,256,512]{2,1,0:T(8,128)} %pad_maximum_fusion.y_ref, f32[512,512]{1,0:T(8,128)} %all-reduce.2.cloned.1.call-done.gram_ref, f32[4,128,128]{2,1,0:T(8,128)} %t_ref.1), custom_call_target="tpu_custom_call" | custom-call | tf_op jit(solution)/shard_map/finish/pallas_call | solution.py:434
  542.3 10.3 %copy.6 = f32[64,49152]{1,0:T(8,128)} copy(f32[64,49152]{1,0:T(8,128)} %finish.1) | data formatting | bytes 25165824
Async XLA Ops:
  6.5 347.9 %all-reduce.2.cloned.1.call-start = ((), (), s32[]{:S(2)}) async-start(), calls=%async_computation | async-start | bytes 2097152 | tf_op jit(solution)/shard_map/psum | solution.py:468
  324.1 6.3 %copy-start.2 = (f32[1,4,64,3072]{3,2,1,0:T(8,128)S(1)}, f32[1,4,64,3072]{3,2,1,0:T(8,128)}, u32[]{:S(2)}) copy-start(f32[1,4,64,3072]{3,2,1,0:T(8,128)} %get-tuple-element.13) | copy-start | bytes 9437188
  330.4 5.5 copy-start.1
  335.9 5.7 %copy-start = (f32[1,4,64,3072]{3,2,1,0:T(8,128)S(1)}, f32[1,4,64,3072]{3,2,1,0:T(8,128)}, u32[]{:S(2)}) copy-start(f32[1,4,64,3072]{3,2,1,0:T(8,128)} %get-tuple-element.9) | copy-start | bytes 9437188
  348.1 5.3 copy-start.3
Sparse Core Ops, SparseCore 0:
  21.5 223.2 all-reduce.1

commit v3 on v2

--- a/solution.py
+++ b/solution.py
@@ -9,7 +9,10 @@
 
 MESH = pl.DeviceIdType.MESH
 GROUP = 4
-CHUNKS = 4
+
+
+def chunks_of(depth):
+    return 4 if depth % 512 == 0 else 1
 
 
 def matmul(left, right, precision=lax.Precision.HIGHEST):
@@ -29,16 +32,25 @@
     return jnp.clip(plane, piece - reach, piece + reach)
 
 
-def spread_kernel(line, slab_ref, vec_ref, xr, vall, xsend, xrecv, vright, vleft, vrecv, own_sem):
+def split(value):
+    coarse = value.astype(jnp.bfloat16)
+    return coarse, (value - coarse.astype(jnp.float32)).astype(jnp.bfloat16)
+
+
+def spread_kernel(
+    line, slab_ref, vec_ref, xr, vall, y_ref,
+    xtile, vtile, xsend, xrecv, vright, vleft, vrecv, own_sem, xload, vload,
+):
     count = line * GROUP
     row, me = lax.axis_index("prow"), lax.axis_index("pcol")
     z, q = me // GROUP, lax.rem(me, GROUP)
     depth = vec_ref.shape[0]
-    part = depth // CHUNKS
+    chunks = chunks_of(depth)
+    part = depth // chunks
     greet_all(count)
 
     def vcopy(source, chunk, to, src, sems):
-        rows = pl.ds(chunk * part, part)
+        rows = pl.ds(pl.multiple_of(chunk * part, part), part)
         return pltpu.make_async_remote_copy(
             src_ref=src.at[rows, :],
             dst_ref=vall.at[source, rows, :],
@@ -48,7 +60,7 @@
             device_id_type=MESH,
         )
 
-    for chunk in range(CHUNKS):
+    for chunk in range(chunks):
         @pl.when(z < line - 1)
         def _():
             vcopy(z, chunk, z + 1, vec_ref, vright).start()
@@ -98,25 +110,25 @@
                 def _():
                     xlocal(piece).start()
 
-    for distance in range(1, line - 1):
-        for chunk in range(CHUNKS):
+    for distance in range(1, line - 2):
+        for chunk in range(chunks):
             @pl.when(z - distance >= 0)
             def _():
                 source = z - distance
                 vcopy(source, chunk, z, vall.at[source], vright).wait_recv()
-                if distance + 1 <= line - 2:
-                    @pl.when(z < line - 1)
-                    def _():
-                        vcopy(source, chunk, z + 1, vall.at[source], vright).start()
+
+                @pl.when(z < line - 1)
+                def _():
+                    vcopy(source, chunk, z + 1, vall.at[source], vright).start()
 
             @pl.when(z + distance <= line - 1)
             def _():
                 source = z + distance
                 vcopy(source, chunk, z, vall.at[source], vleft).wait_recv()
-                if distance + 1 <= line - 2:
-                    @pl.when(z > 0)
-                    def _():
-                        vcopy(source, chunk, z - 1, vall.at[source], vleft).start()
+
+                @pl.when(z > 0)
+                def _():
+                    vcopy(source, chunk, z - 1, vall.at[source], vleft).start()
 
     own.wait()
 
@@ -137,10 +149,68 @@
             for step in range(1, GROUP):
                 xarrived(piece, lax.rem(q + step, GROUP))
 
-    @pl.when(jnp.logical_or(z == 1, z == line - 2))
+    def load(slot, piece, chunk):
+        span = pl.ds(pl.multiple_of(chunk * part, part), part)
+        return (
+            pltpu.make_async_copy(xr.at[slot, :, :, span], xtile, xload),
+            pltpu.make_async_copy(vall.at[piece, span, :], vtile, vload),
+        )
+
+    def accumulate(kind):
+        left, left_fine = split(xtile[...].reshape(GROUP * xtile.shape[1], part))
+        right, right_fine = split(vtile[...])
+        dot = functools.partial(jnp.dot, preferred_element_type=jnp.float32)
+        y_ref[kind] += dot(left, right) + (dot(left_fine, right) + dot(left, right_fine))
+
+    y_ref[...] = jnp.zeros_like(y_ref)
+
+    def near_body(index, carry):
+        piece = index // chunks
+
+        @pl.when(jnp.logical_and(piece - z < line - 2, z - piece < line - 2))
+        def _():
+            loads = load(piece, piece, lax.rem(index, chunks))
+            for copy in loads:
+                copy.start()
+            for copy in loads:
+                copy.wait()
+            accumulate(0)
+
+        return carry
+
+    lax.fori_loop(0, line * chunks, near_body, 0)
+
+    helps = jnp.logical_or(z == 1, z == line - 2)
+
+    @pl.when(helps)
     def _():
         for other in range(GROUP):
             xarrived(line, other)
+
+    @pl.when(jnp.logical_or(z <= 1, z >= line - 2))
+    def _():
+        last = jnp.where(z <= 1, z + line - 2, z - line + 2)
+
+        def last_body(chunk, carry):
+            vcopy(last, chunk, z, vec_ref, vright).wait_recv()
+            loads = load(last, last, chunk)
+            for copy in loads:
+                copy.start()
+            for copy in loads:
+                copy.wait()
+            accumulate(0)
+
+            @pl.when(helps)
+            def _():
+                span = pl.ds(pl.multiple_of(chunk * part, part), part)
+                again = pltpu.make_async_copy(xr.at[line, :, :, span], xtile, xload)
+                again.start()
+                again.wait()
+                accumulate(1)
+
+            return carry
+
+        lax.fori_loop(0, chunks, last_body, 0)
 
     for piece in range(line):
         for step in range(1, GROUP):
@@ -151,7 +221,7 @@
             xremote(piece, 0).wait_send()
 
     for distance in range(0, line - 2):
-        for chunk in range(CHUNKS):
+        for chunk in range(chunks):
             @pl.when(jnp.logical_and(z - distance >= 0, z < line - 1))
             def _():
                 vcopy(z - distance, chunk, z + 1, vec_ref, vright).wait_send()
@@ -164,30 +234,33 @@
 def spread(line, slab, vectors):
     rows = slab.shape[0]
     depth, width = vectors.shape
+    chunks = chunks_of(depth)
     return pl.pallas_call(
         functools.partial(spread_kernel, line),
         out_shape=(
             jax.ShapeDtypeStruct((line + 1, GROUP, rows, depth), jnp.float32),
             jax.ShapeDtypeStruct((line, depth, width), jnp.float32),
+            jax.ShapeDtypeStruct((2, GROUP * rows, width), jnp.float32),
         ),
         in_specs=[pl.BlockSpec(memory_space=pl.ANY)] * 2,
-        out_specs=(pl.BlockSpec(memory_space=pl.ANY),) * 2,
+        out_specs=(pl.BlockSpec(memory_space=pl.ANY),) * 2 + (pl.BlockSpec(memory_space=pltpu.VMEM),),
         scratch_shapes=[
+            pltpu.VMEM((GROUP, rows, depth // chunks), jnp.float32),
+            pltpu.VMEM((depth // chunks, width), jnp.float32),
             pltpu.SemaphoreType.DMA((line, GROUP)),
             pltpu.SemaphoreType.DMA((line + 1, GROUP)),
-            pltpu.SemaphoreType.DMA((line, CHUNKS)),
-            pltpu.SemaphoreType.DMA((line, CHUNKS)),
-            pltpu.SemaphoreType.DMA((line, CHUNKS)),
+            pltpu.SemaphoreType.DMA((line, chunks)),
+            pltpu.SemaphoreType.DMA((line, chunks)),
+            pltpu.SemaphoreType.DMA((line, chunks)),
+            pltpu.SemaphoreType.DMA,
+            pltpu.SemaphoreType.DMA,
             pltpu.SemaphoreType.DMA,
         ],
-        compiler_params=pltpu.CompilerParams(collective_id=0, has_side_effects=True),
+        compiler_params=pltpu.CompilerParams(
+            collective_id=0, has_side_effects=True, vmem_limit_bytes=40 * 1024 * 1024
+        ),
         name="spread",
     )(slab, vectors)
-
-
-def split(value):
-    coarse = value.astype(jnp.bfloat16)
-    return coarse, (value - coarse.astype(jnp.float32)).astype(jnp.bfloat16)
 
 
 def across(left, right):
@@ -197,7 +270,7 @@
 def finish_kernel(
     line, lanes, x_ref, v_ref, y_ref, gram_ref, t_ref, out_ref,
     xbuf, vbuf, inbox, total, wbox, wsplit,
-    xload, vload, ysend, yrecv, wsend, wrecv, send, recv,
+    xload, vload, ysend, yrecv, wsend, wrecv, send, recv, handed,
 ):
     row, me = lax.axis_index("prow"), lax.axis_index("pcol")
     z, q = me // GROUP, lax.rem(me, GROUP)
@@ -221,8 +294,17 @@
     def others():
         return [lax.rem(mine + step, members) for step in range(1, members)]
 
+    def near(piece):
+        return place_of(line, z, piece) == z
+
+    def xarrive(slot):
+        return pltpu.make_async_copy(x_ref.at[slot], xbuf.at[slot], xload.at[slot])
+
     for slot in range(line + 1):
-        pltpu.make_async_copy(x_ref.at[slot], xbuf.at[slot], xload.at[slot]).start()
+        @pl.when(near(slot) if slot < line else helps)
+        def _():
+            xarrive(slot).start()
+
     for piece in range(line):
         pltpu.make_async_copy(v_ref.at[piece], vbuf.at[piece], vload.at[piece]).start()
 
@@ -283,7 +365,7 @@
     for k in reversed(range(blocks)):
         now = total[:, k * width : (k + 1) * width]
         for j in done:
-            now = now - matmul(done[j], gram_ref[j * width : (j + 1) * width, k * width : (k + 1) * width])
+            now = now - matmul(done[j], gram_ref[(j - 1) * width : j * width, k * width : (k + 1) * width])
         done[k] = lax.dot_general(
             now, t_ref[k], (((1,), (1,)), ((), ())),
             precision=lax.Precision.HIGHEST, preferred_element_type=jnp.float32,
@@ -319,11 +401,11 @@
     for other in others():
         wcopy(0, z, other).start()
 
-    def xarrive(slot):
-        pltpu.make_async_copy(x_ref.at[slot], xbuf.at[slot], xload.at[slot]).wait()
-
     for slot in range(line + 1):
-        xarrive(slot)
+        @pl.when(near(slot) if slot < line else helps)
+        def _():
+            xarrive(slot).wait()
+
     for piece in range(line):
         pltpu.make_async_copy(v_ref.at[piece], vbuf.at[piece], vload.at[piece]).wait()
 
@@ -346,21 +428,37 @@
     def columns(piece, other):
         return pl.ds(pl.multiple_of((piece * GROUP + other) * depth, 128), depth)
 
-    def remote(slot, piece, plane, other):
+    def remote(piece, other):
         return pltpu.make_async_remote_copy(
-            src_ref=xbuf.at[slot, other],
+            src_ref=xbuf.at[piece, other],
             dst_ref=out_ref.at[:, columns(piece, q)],
-            send_sem=send.at[slot, other],
+            send_sem=send.at[piece, other],
             recv_sem=recv.at[piece, q],
-            device_id=(row, plane * GROUP + other),
+            device_id=(row, z * GROUP + other),
             device_id_type=MESH,
         )
 
     def local(piece):
         return pltpu.make_async_copy(xbuf.at[piece, q], out_ref.at[:, columns(piece, q)], recv.at[piece, q])
 
-    def near(piece):
-        return place_of(line, z, piece) == z
+    def hand(group, plane):
+        return pltpu.make_async_remote_copy(
+            src_ref=xbuf.at[line, group],
+            dst_ref=xbuf.at[far_piece, group],
+            send_sem=send.at[line, group],
+            recv_sem=handed.at[group],
+            device_id=(row, plane * GROUP + q),
+            device_id_type=MESH,
+        )
+
+    @pl.when(helps)
+    def _():
+        for other in range(members):
+            warrived(1, other)
+        wsplit[2], wsplit[3] = split(wbox[1])
+        update(line, far_piece, 1)
+        for group in range(GROUP):
+            hand(group, far_plane).start()
 
     for other in others():
         warrived(0, other)
@@ -371,18 +469,21 @@
         def _():
             update(piece, piece, 0)
             for step in (1, 2, 3):
-                remote(piece, piece, z, lax.rem(q + step, GROUP)).start()
+                remote(piece, lax.rem(q + step, GROUP)).start()
             local(piece).start()
 
-        if piece == 0:
-            @pl.when(helps)
-            def _():
-                for other in range(members):
-                    warrived(1, other)
-                wsplit[2], wsplit[3] = split(wbox[1])
-                update(line, far_piece, 1)
-                for other in range(GROUP):
-                    remote(line, far_piece, far_plane, other).start()
+    @pl.when(ends)
+    def _():
+        for group in range(GROUP):
+            hand(group, z).wait_recv()
+
+            @pl.when(q == group)
+            def _():
+                local(far_piece).start()
+
+            @pl.when(q != group)
+            def _():
+                remote(far_piece, group).start()
 
     def arrived(piece, other):
         pltpu.make_async_remote_copy(
@@ -395,18 +496,10 @@
         ).wait_recv()
 
     for piece in range(line):
+        local(piece).wait()
         for step in range(1, GROUP):
             arrived(piece, lax.rem(q + step, GROUP))
-
-        @pl.when(near(piece))
-        def _():
-            local(piece).wait()
-            for step in range(1, GROUP):
-                remote(piece, piece, z, lax.rem(q + step, GROUP)).wait_send()
-
-        @pl.when(jnp.logical_not(near(piece)))
-        def _():
-            arrived(piece, q)
+            remote(piece, lax.rem(q + step, GROUP)).wait_send()
 
     for other in others():
         ycopy(0, z, other).wait_send()
@@ -421,8 +514,8 @@
     def _():
         for other in range(members):
             ycopy(1, far_plane, other).wait_send()
-        for other in range(GROUP):
-            remote(line, far_piece, far_plane, other).wait_send()
+        for group in range(GROUP):
+            hand(group, far_plane).wait_send()
 
 
 def finish(line, lanes, x, v, y, gram, tfactors):
@@ -451,6 +544,7 @@
             dma((2 * members,)),
             dma((line + 1, GROUP)),
             dma((line, GROUP)),
+            dma((GROUP,)),
         ],
         compiler_params=pltpu.CompilerParams(
             collective_id=1, has_side_effects=True, vmem_limit_bytes=60 * 1024 * 1024
@@ -460,23 +554,10 @@
 
 
 def per_device(line, lanes, slab, vectors, tfactors):
-    rows = slab.shape[0]
-    depth, total = vectors.shape
-    z = lax.axis_index("pcol") // GROUP
-    high = lax.Precision.HIGH
-
-    gram = lax.psum(matmul(vectors.T, vectors, high), ("prow", "pcol"))
-    blocks, vall = spread(line, slab, vectors)
-    xr = blocks.reshape(line + 1, GROUP * rows, depth)
-
-    own = jnp.zeros((GROUP * rows, total), jnp.float32)
-    for piece in range(line):
-        near = place_of(line, z, piece) == z
-        own = own + jnp.where(near, matmul(xr[piece], vall[piece], high), 0.0)
-    far_piece = jnp.where(z <= 1, line - 1, 0)
-    far_vectors = lax.dynamic_index_in_dim(vall, far_piece, 0, keepdims=False)
-    extra = matmul(xr[line], far_vectors, high)
-    return finish(line, lanes, blocks, vall, jnp.stack([own, extra]), gram, tfactors)
+    width = tfactors.shape[1]
+    gram = lax.psum(matmul(vectors[:, width:].T, vectors[:, :-width], lax.Precision.HIGH), ("prow", "pcol"))
+    blocks, vall, products = spread(line, slab, vectors)
+    return finish(line, lanes, blocks, vall, products, gram, tfactors)
 
 
 def solution(mesh):

time: 560 us -> 500 us (0.89)
  matrix products: 44 us -> 8.46 us
  Pallas kernels: 480 us -> 459 us
  local copies, waits for them, and re-layouts: 21.2 us -> 14 us
    dot_general x6 -> x1, matrix products: 44 us -> 8.46 us  [matmul(): jnp.dot(left, right, precision=precision, preferred_element_type=jnp.floa...]
    pallas_call x1, Pallas kernels: 188 us -> 170 us  [finish(): pl.pallas_call(functools.partial(finish_kernel, line, lanes), out_shape=j...]
    slice x1 -> x0, local copies, waits for them, and re-layouts: 10.9 us -> none  [per_device(): own = own + jnp.where(near, matmul(xr[piece], vall[piece], high), 0.0)]
    unnamed x9 -> x5, local copies, waits for them, and re-layouts: 10.3 us -> 14 us
  transfers between devices with their start and end apart: 1 -> 1, of which waited for: 0 -> 0; matrix products, arithmetic and copies ran while one was open for 7% -> 0% of each run, Pallas kernels for 52% -> 58%
where the time goes in v3:
time: 500 us; the launch traced here: 495 us
  Pallas kernels  459 us (92%)
  local copies, waits for them, and re-layouts  14 us (3%)
  between operations  13.4 us (3%)
  matrix products  8.46 us (2%)
    pallas_call x1, Pallas kernels, spread(): pl.pallas_call(functools.partial(spread_kernel, line), out_shape=(jax.Sha...  289 us
    pallas_call x1, Pallas kernels, finish(): pl.pallas_call(functools.partial(finish_kernel, line, lanes), out_shape=j...  170 us
    unnamed x5, local copies, waits for them, and re-layouts  14 us
  transfers between devices with their start and end apart: 1, of which 0 were waited for; matrix products, arithmetic and copies ran while one was open for 0% of the time, Pallas kernels for 58%

profile of v3, /device:TPU:0, one launch (start us, length us, event | category | flops | bytes accessed | tf_op | source)
XLA Modules:
  0.0 494.7 jit_solution(7882075292629496987)
XLA Ops:
  6.5 0.0 all-reduce.2.cloned.1.call-start
  6.5 8.5 %fusion = f32[384,384]{1,0:T(8,128)} fusion(f32[3072,512]{1,0:T(8,128)} %vec_ref.1), kind=kOutput, calls=%fused_computation | convolution fusion | flops 2717908992 | bytes 10027008 | tf_op jit(solution)/shard_map/dot_general | solution.py:19
  15.0 0.0 all-reduce.2.cloned.1.call-update
  15.0 0.0 copy-start
  15.0 2.8 copy-done
  17.8 289.2 %spread.1 = (f32[5,4,64,3072]{3,2,1,0:T(8,128)}, f32[4,3072,512]{2,1,0:T(8,128)}, f32[2,256,512]{2,1,0:T(8,128)S(1)}) custom-call(f32[64,49152]{1,0:T(8,128)} %slab_ref.1, f32[3072,512]{1,0:T(8,128)S(1)} %copy-done), custom_call_target="tpu_custom_call" | custom-call | tf_op jit(solution)/shard_map/spread/pallas_call | solution.py:238
  307.0 0.0 copy-start.1
  307.1 1.0 copy-done.1
  308.0 0.0 all-reduce.2.cloned.1.call-done.gram_ref
  308.0 169.5 %finish.1 = f32[64,49152]{1,0:T(8,128)} custom-call(f32[5,4,64,3072]{3,2,1,0:T(8,128)} %get-tuple-element.8.x_ref, f32[4,3072,512]{2,1,0:T(8,128)} %get-tuple-element.9.v_ref, f32[2,256,512]{2,1,0:T(8,128)} %copy-done.1, f32[384,384]{1,0:T(8,128)} %all-reduce.2.cloned.1.call-done.gram_ref, f32[4,128,128]{2,1,0:T(8,128)} %t_ref.1), custom_call_target="tpu_custom_call" | custom-call | tf_op jit(solution)/shard_map/finish/pallas_call | solution.py:527
  477.6 10.3 %copy.6 = f32[64,49152]{1,0:T(8,128)} copy(f32[64,49152]{1,0:T(8,128)} %finish.1) | data formatting | bytes 25165824
Async XLA Ops:
  6.5 301.5 %all-reduce.2.cloned.1.call-start = ((), (), s32[]{:S(2)}) async-start(), calls=%async_computation | async-start | bytes 1179648 | tf_op jit(solution)/shard_map/psum | solution.py:558
  15.0 2.8 copy-start
  307.0 1.0 copy-start.1
Sparse Core Ops, SparseCore 0:
  15.1 254.9 all-reduce.1
